TPU v7x, 512 devices: a whole 4x8x8 slice. The times are simulated.
512 devices in a mesh: layer: 4 (over x), seq: 16 (over y, core), tile: 8 (over z).
Axes of the slice: x: 4, y: 8, z: 8, core: 2. Of those that a mesh axis runs over, the one named last changes fastest.
Arguments:
- activations: bfloat16 [16, 3072, 4096], P('layer', 'seq', 'tile'), parts along dimension 0, may hold values from -6 to 6
- out_grads: bfloat16 [16, 3072, 14336], P('layer', 'seq', 'tile'), parts along dimension 0, may hold values from -6 to 6
- proj_in: bfloat16 [16384, 128], P(('layer', 'tile')), parts along dimension 0, may hold values from -0.09375 to 0.09375
- proj_out: bfloat16 [57344, 256], P(('layer', 'tile')), parts along dimension 0, may hold values from -0.046875 to 0.046875
- seq_lengths: int32 [4], replicated, may hold values from 1 to 3072, 7680 in all
- tile_map: int32 [128, 2], replicated, may hold values from 0 to 127, as said below
- prior_cov: float32 [512, 256, 256], P(('layer', 'seq', 'tile')), parts along dimension 0, may hold values from -6 to 6
Outputs:
- covariance: float32 [512, 256, 256], P(('layer', 'seq', 'tile')), parts along dimension 0
There are 4 independent parts, one for each index of `layer`. A program takes and returns all parts, laid end to end along the dimension named above; an argument that names none is the same for every part. Nothing has to cross between parts.
Inputs may be any that keep to these rules, and one draw needn't show every extreme that they name: `tile_map`: each row holds two feature block numbers, the first not above the second; rows may repeat.
All inputs are finite; a program needn't handle non-finite values.
Results may differ from a plain program's by a relative error of at most 0.0003.
Values sent between devices are 32-bit elements; how exact they have to be, the bound alone decides.
No kernel may reach another device: no remote copies, remote signals or barrier semaphores. Data moves between devices by JAX's collectives and lax.ppermute only.
A program may use at most 192 MiB of HBM per device.

v0:
```python
import jax
import jax.numpy as jnp
from jax import lax
from jax.sharding import PartitionSpec as P


def project_tokens(act_rows, grad_rows, proj_in, proj_out):
    left_side = jnp.einsum("slc,ck->lsk", act_rows, proj_in, preferred_element_type=jnp.float32)
    right_side = jnp.einsum("slc,ck->lsk", grad_rows, proj_out, preferred_element_type=jnp.float32)
    return jnp.concatenate([left_side, right_side], axis=2)


def body(activations, out_grads, proj_in, proj_out, seq_lengths, tile_map, prior_cov):
    tiles_here = prior_cov.shape[0]
    block_size = prior_cov.shape[1]
    seq_count = activations.shape[0]
    tok_len = activations.shape[1]
    width_in = proj_in.shape[1]
    width_out = proj_out.shape[1]
    tile_count = lax.axis_size("tile")
    tok_rows = tok_len // tile_count
    whole_term = project_tokens(activations, out_grads, proj_in, proj_out)
    totals = lax.psum(whole_term, "tile")
    summed = lax.dynamic_slice_in_dim(totals, lax.axis_index("tile") * tok_rows, tok_rows, 0)
    positions = (
        lax.axis_index("seq") * tok_len
        + lax.axis_index("tile") * tok_rows
        + jnp.arange(tok_rows, dtype=jnp.int32)
    )
    token_mask = (positions[:, None] < seq_lengths[None, :]).astype(jnp.float32)
    token_weight = token_mask * lax.rsqrt(seq_lengths.astype(jnp.float32))[None, :]
    left_part = summed[:, :, :width_in]
    right_part = summed[:, :, width_in:] * token_weight[:, :, None]
    partial_value = jnp.einsum(
        "lsj,lsi->sji", right_part, left_part, precision=lax.Precision.HIGHEST
    )
    partial_value = partial_value.reshape(seq_count, width_out * width_in)
    offsets = jnp.arange(block_size, dtype=jnp.int32)
    features = lax.psum_scatter(partial_value, ("seq", "tile"), scatter_dimension=1, tiled=True)
    owner_index = lax.axis_index(("seq", "tile"))
    own_pairs = lax.dynamic_slice_in_dim(tile_map, owner_index * tiles_here, tiles_here, 0)
    shard_piece = lax.all_gather(features, ("seq", "tile"), axis=1, tiled=True)
    piece_width = shard_piece.shape[1]
    columns = own_pairs[:, :, None] * block_size + offsets
    inside = (columns >= 0) & (columns < piece_width)
    picked = jnp.take(shard_piece, jnp.clip(columns, 0, piece_width - 1), axis=1)
    picked = jnp.where(inside[None], picked, 0.0)
    chosen = jnp.transpose(picked, (1, 2, 0, 3))
    product = jnp.einsum(
        "kse,ksf->kef", chosen[:, 0], chosen[:, 1], precision=lax.Precision.HIGHEST
    )
    return prior_cov + product


def solution(mesh):
    return jax.shard_map(
        body,
        mesh=mesh,
        in_specs=(
            P("layer", "seq", "tile"),
            P("layer", "seq", "tile"),
            P(("layer", "tile"), None),
            P(("layer", "tile"), None),
            P(),
            P(),
            P(("layer", "seq", "tile"), None, None),
        ),
        out_specs=P(("layer", "seq", "tile"), None, None),
        check_vma=False,
    )
```

profile of v0, /device:TPU:25, one launch (start us, length us, event | category | flops | bytes accessed | tf_op | source)
XLA Modules:
  0.0 484.0 jit_solution(7159621079205856472)
XLA Ops:
  6.5 0.0 copy-start
  6.5 1.8 copy-done
  8.3 2.1 convolution_bitcast_fusion
  10.4 0.0 copy-done.1
  10.4 0.0 copy-done.3
  10.4 0.4 convolution_bitcast_fusion.1
  10.8 1.1 pad_maximum_fusion
  11.9 0.0 all-reduce.2.cloned.1.call-update
  12.0 0.0 reduce-scatter.2.cloned.1.call-start
  12.0 0.6 copy-done.5
  12.6 0.1 compare_select_fusion.2
  12.7 82.7 %all-reduce.2.cloned.1.call-done = f32[192,4,384]{2,0,1:T(8,128)} async-done(((f32[192,4,384]{2,0,1:T(8,128)}), f32[192,4,384]{2,0,1:T(8,128)}) %all-reduce.2.cloned.1.call-update) | async-done | bytes 1179664 | tf_op jit(solution)/shard_map/psum | solution.py:23
  95.4 2.0 fusion.3
  97.4 8.7 %copy.10 = f32[4,256,128]{0,2,1:T(8,128)} copy(f32[4,256,128]{2,1,0:T(8,128)S(1)} %fusion.3) | data formatting | bytes 1048576 | tf_op jit(solution)/shard_map/reshape | solution.py:37
  106.1 0.0 reduce-scatter.2.cloned.1.call-update
  106.1 0.6 copy-done.4
  106.7 0.2 multiply_reduce_fusion
  106.9 0.1 fusion.6
  107.0 0.1 compare_and_fusion.1
  107.1 220.6 %reduce-scatter.2.cloned.1.call-done = f32[4,256]{0,1:T(8,128)} async-done(((f32[4,32768]{0,1:T(8,128)}), f32[4,256]{0,1:T(8,128)}) %reduce-scatter.2.cloned.1.call-update) | async-done | bytes 4112 | tf_op jit(solution)/shard_map/reduce_scatter | solution.py:39
  327.7 141.3 %all_gather.3 = f32[4,32768]{0,1:T(8,128)} all-gather(f32[4,256]{0,1:T(8,128)} %reduce-scatter.2.cloned.1.call-done), channel_id=1, replica_groups=mesh['layer'=4,'seq'=16,'tile'=8] {'seq','tile'}, dimensions={1}, use_global_device_ids=true | all-gather | bytes 528384 | tf_op jit(solution)/shard_map/all_gather | solution.py:42
  469.0 6.8 %gather_fusion = f32[512,4]{1,0:T(8,128)S(1)} fusion(f32[4,32768]{0,1:T(8,128)} %all_gather.3, s32[1024]{0:T(1024)S(1)} %pad_clamp_fusion), kind=kCustom, calls=%fused_computation | custom fusion | bytes 18432 | tf_op jit(solution)/shard_map/jit(_take)/gather | solution.py:46
  475.8 0.2 select_bitcast_fusion
  476.0 1.1 fusion
  (11 shorter events, 0.0 us)
Async XLA Ops:
  6.5 1.8 copy-start
  6.5 3.9 copy-start.1
  6.5 88.8 %all-reduce.2.cloned.1.call-start = ((), (), s32[]{:S(2)}) async-start(), calls=%async_computation.1 | async-start | bytes 2359296 | tf_op jit(solution)/shard_map/psum | solution.py:23
  8.3 2.1 copy-start.3
  11.9 0.7 copy-start.5
  12.0 315.8 %reduce-scatter.2.cloned.1.call-start = ((), (), s32[]{:S(2)}) async-start(), calls=%async_computation.2 | async-start | bytes 16908288 | tf_op jit(solution)/shard_map/reduce_scatter | solution.py:39
  106.1 0.7 copy-start.4
  107.1 368.9 %copy-start.2 = (f32[1,256,256]{2,1,0:T(8,128)S(1)}, f32[1,256,256]{2,1,0:T(8,128)}, u32[]{:S(2)}) copy-start(f32[1,256,256]{2,1,0:T(8,128)} %param.13) | copy-start | bytes 786436
Sparse Core Ops, SparseCore 0:
  12.1 83.2 all-reduce.1
  106.2 221.4 reduce-scatter.1
where the time goes:
time: 484 us
  waiting for transfers between devices  303 us (63%)
  blocking collectives  141 us (29%)
  local copies, waits for them, and re-layouts  18.5 us (4%)
  between operations  13.5 us (3%)
  matrix products  5.57 us (1%)
    reduce_scatter x1, waiting for transfers between devices, body(): lax.psum_scatter(partial_value, ('seq', 'tile'), scatter_dimension=1, til...  221 us
    all_gather x1, blocking collectives, body(): shard_piece = lax.all_gather(features, ('seq', 'tile'), axis=1, tiled=True)  141 us
    psum x1, waiting for transfers between devices, body(): totals = lax.psum(whole_term, 'tile')  82.7 us
  transfers between devices with their start and end apart: 2, of which 2 were waited for; matrix products, arithmetic and copies ran while one was open for 0% of the time, Pallas kernels for 0%

commit v1 on v0

--- a/solution.py
+++ b/solution.py
@@ -20,7 +20,9 @@
     tile_count = lax.axis_size("tile")
     tok_rows = tok_len // tile_count
     whole_term = project_tokens(activations, out_grads, proj_in, proj_out)
-    totals = lax.psum(whole_term, "tile")
+    totals = whole_term
+    for hop in (1, 2, 4):
+        totals = totals + lax.ppermute(totals, "tile", [(dev, dev ^ hop) for dev in range(8)])
     summed = lax.dynamic_slice_in_dim(totals, lax.axis_index("tile") * tok_rows, tok_rows, 0)
     positions = (
         lax.axis_index("seq") * tok_len

time: 484 us -> 546 us (1.13)
  the two profiles are of different devices: /device:TPU:25 before, /device:TPU:2 now
where the time goes in v1:
time: 546 us; the launch traced here: 545 us
  waiting for transfers between devices  351 us (64%)
  blocking collectives  137 us (25%)
  starting transfers between devices  18.8 us (3%)
  local copies, waits for them, and re-layouts  17.9 us (3%)
  between operations  13.5 us (2%)
    reduce_scatter x1, waiting for transfers between devices, body(): lax.psum_scatter(partial_value, ('seq', 'tile'), scatter_dimension=1, til...  223 us
    all_gather x1, blocking collectives, body(): shard_piece = lax.all_gather(features, ('seq', 'tile'), axis=1, tiled=True)  137 us
    ppermute x3, waiting for transfers between devices, body(): lax.ppermute(totals, 'tile', [(dev, dev ^ hop) for dev in range(8)])  128 us
    ppermute x3, starting transfers between devices, body(): lax.ppermute(totals, 'tile', [(dev, dev ^ hop) for dev in range(8)])  18.8 us
  transfers between devices with their start and end apart: 4, of which 4 were waited for; matrix products, arithmetic and copies ran while one was open for 0% of the time, Pallas kernels for 0%

profile of v1, /device:TPU:2, one launch (start us, length us, event | category | flops | bytes accessed | tf_op | source)
XLA Modules:
  0.0 545.4 jit_solution(15329065363934360973)
XLA Ops:
  6.5 1.8 copy-done
  8.3 2.1 convolution_bitcast_fusion
  10.4 0.4 convolution_bitcast_fusion.1
  10.8 0.1 pad_maximum_fusion
  10.9 4.3 collective-permute-start
  15.2 26.0 %collective-permute-done = f32[192,4,384]{2,0,1:T(8,128)S(1)} collective-permute-done((f32[192,4,384]{2,0,1:T(8,128)S(1)}, f32[192,4,384]{2,0,1:T(8,128)S(1)}, u32[]{:S(2)}, u32[]{:S(2)}) %collective-permute-start) | collective-permute-done | bytes 1179680 | tf_op jit(solution)/shard_map/ppermute | solution.py:25
  41.1 0.1 fusion.7
  41.3 6.1 %collective-permute-start.1 = (f32[192,4,384]{2,0,1:T(8,128)S(1)}, f32[192,4,384]{2,0,1:T(8,128)S(1)}, u32[]{:S(2)}, u32[]{:S(2)}) collective-permute-start(f32[192,4,384]{2,0,1:T(8,128)S(1)} %fusion.7), channel_id=1, source_target_pairs={{0,2},{1,3},{2,0},{3,1},{4,6},{5,7},{6,4},{7,5},{8,10},{9,11},{10,... | collective-permute-start | bytes 3538952 | tf_op jit(solution)/shard_map/ppermute | solution.py:25
  47.4 50.7 %collective-permute-done.1 = f32[192,4,384]{2,0,1:T(8,128)S(1)} collective-permute-done((f32[192,4,384]{2,0,1:T(8,128)S(1)}, f32[192,4,384]{2,0,1:T(8,128)S(1)}, u32[]{:S(2)}, u32[]{:S(2)}) %collective-permute-start.1) | collective-permute-done | bytes 1179680 | tf_op jit(solution)/shard_map/ppermute | solution.py:25
  98.1 1.1 add.109
  99.2 8.4 %collective-permute-start.2 = (f32[192,4,384]{2,0,1:T(8,128)}, f32[192,4,384]{2,0,1:T(8,128)}, u32[]{:S(2)}, u32[]{:S(2)}) collective-permute-start(f32[192,4,384]{2,0,1:T(8,128)} %add.109), channel_id=1, source_target_pairs={{0,4},{1,5},{2,6},{3,7},{4,0},{5,1},{6,2},{7,3},{8,12},{9,13},{10,... | collective-permute-start | bytes 3538952 | tf_op jit(solution)/shard_map/ppermute | solution.py:25
  107.7 51.1 %collective-permute-done.2 = f32[192,4,384]{2,0,1:T(8,128)} collective-permute-done((f32[192,4,384]{2,0,1:T(8,128)}, f32[192,4,384]{2,0,1:T(8,128)}, u32[]{:S(2)}, u32[]{:S(2)}) %collective-permute-start.2) | collective-permute-done | bytes 1179680 | tf_op jit(solution)/shard_map/ppermute | solution.py:25
  158.8 1.0 dynamic-slice_add_fusion
  159.8 1.1 fusion.3
  161.0 8.7 %copy.10 = f32[4,256,128]{0,2,1:T(8,128)} copy(f32[4,256,128]{2,1,0:T(8,128)S(1)} %fusion.3) | data formatting | bytes 1048576 | tf_op jit(solution)/shard_map/reshape | solution.py:39
  169.7 0.6 copy-done.4
  170.3 0.2 multiply_reduce_fusion
  170.5 0.1 fusion.6
  170.6 0.1 compare_and_fusion.1
  170.7 222.9 %reduce-scatter.2.cloned.1.call-done = f32[4,256]{0,1:T(8,128)} async-done(((f32[4,32768]{0,1:T(8,128)}), f32[4,256]{0,1:T(8,128)}) %reduce-scatter.2.cloned.1.call-update) | async-done | bytes 4112 | tf_op jit(solution)/shard_map/reduce_scatter | solution.py:41
  393.6 136.8 %all_gather.3 = f32[4,32768]{0,1:T(8,128)} all-gather(f32[4,256]{0,1:T(8,128)} %reduce-scatter.2.cloned.1.call-done), channel_id=1, replica_groups=mesh['layer'=4,'seq'=16,'tile'=8] {'seq','tile'}, dimensions={1}, use_global_device_ids=true | all-gather | bytes 528384 | tf_op jit(solution)/shard_map/all_gather | solution.py:44
  530.4 6.8 %gather_fusion = f32[512,4]{1,0:T(8,128)S(1)} fusion(f32[4,32768]{0,1:T(8,128)} %all_gather.3, s32[1024]{0:T(1024)S(1)} %pad_clamp_fusion), kind=kCustom, calls=%fused_computation | custom fusion | bytes 18432 | tf_op jit(solution)/shard_map/jit(_take)/gather | solution.py:48
  537.3 0.2 select_bitcast_fusion
  537.5 1.1 fusion
  (17 shorter events, 0.1 us)
Async XLA Ops:
  6.5 1.8 copy-start
  6.5 3.9 copy-start.1
  6.5 387.1 %reduce-scatter.2.cloned.1.call-start = ((), (), s32[]{:S(2)}) async-start(), calls=%async_computation.1 | async-start | bytes 16908288 | tf_op jit(solution)/shard_map/reduce_scatter | solution.py:41
  8.3 2.1 copy-start.3
  10.9 30.2 %collective-permute-start = (f32[192,4,384]{2,0,1:T(8,128)S(1)}, f32[192,4,384]{2,0,1:T(8,128)S(1)}, u32[]{:S(2)}, u32[]{:S(2)}) collective-permute-start(f32[192,4,384]{2,0,1:T(8,128)S(1)} %pad_maximum_fusion), channel_id=1, source_target_pairs={{0,1},{1,0},{2,3},{3,2},{4,5},{5,4},{6,7},{7,6},{8,9},{9,8},{10,11... | collective-permute-start | bytes 3538952 | tf_op jit(solution)/shard_map/ppermute | solution.py:25
  41.3 66.4 %copy-start.5 = (s32[4]{0:T(128)S(1)}, s32[4]{0:T(128)}, u32[]{:S(2)}) copy-start(s32[4]{0:T(128)} %param.11) | copy-start | bytes 52
  41.3 56.8 %collective-permute-start.1 = (f32[192,4,384]{2,0,1:T(8,128)S(1)}, f32[192,4,384]{2,0,1:T(8,128)S(1)}, u32[]{:S(2)}, u32[]{:S(2)}) collective-permute-start(f32[192,4,384]{2,0,1:T(8,128)S(1)} %fusion.7), channel_id=1, source_target_pairs={{0,2},{1,3},{2,0},{3,1},{4,6},{5,7},{6,4},{7,5},{8,10},{9,11},{10,... | collective-permute-start | bytes 3538952 | tf_op jit(solution)/shard_map/ppermute | solution.py:25
  99.2 59.6 %collective-permute-start.2 = (f32[192,4,384]{2,0,1:T(8,128)}, f32[192,4,384]{2,0,1:T(8,128)}, u32[]{:S(2)}, u32[]{:S(2)}) collective-permute-start(f32[192,4,384]{2,0,1:T(8,128)} %add.109), channel_id=1, source_target_pairs={{0,4},{1,5},{2,6},{3,7},{4,0},{5,1},{6,2},{7,3},{8,12},{9,13},{10,... | collective-permute-start | bytes 3538952 | tf_op jit(solution)/shard_map/ppermute | solution.py:25
  169.7 0.7 copy-start.4
  170.7 366.8 %copy-start.2 = (f32[1,256,256]{2,1,0:T(8,128)S(1)}, f32[1,256,256]{2,1,0:T(8,128)}, u32[]{:S(2)}) copy-start(f32[1,256,256]{2,1,0:T(8,128)} %param.13) | copy-start | bytes 786436
Sparse Core Ops, SparseCore 0:
  169.8 223.7 reduce-scatter.1
